TPU v7x, 32 devices: a whole 2x2x4 slice. The times are simulated.
32 devices in a mesh: row: 8 (over y, x, core), col: 4 (over z).
Axes of the slice: x: 2, y: 2, z: 4, core: 2. Of those that a mesh axis runs over, the one named last changes fastest.
Arguments:
- features: float32 [1536, 256], P(('row', 'col')), may hold values from -6 to 6
- inv_scale: float32 [256], replicated, may hold values from 0.001953125 to 0.015625
- probe_u: float32 [1536, 64], P(('row', 'col')), may hold values from -6 to 6
- solve_v: float32 [1536, 64], P(('row', 'col')), may hold values from -6 to 6
Outputs:
- feature_grad: float32 [1536, 256], P(('row', 'col'))
All inputs are finite; a program needn't handle non-finite values.
Results may differ from a plain program's by a relative error of at most 0.0003.
Values sent between devices are 32-bit elements; how exact they have to be, the bound alone decides.
A program may use at most 64 MiB of HBM per device.

v0:
```python
import jax
import jax.numpy as jnp
from jax import lax
from jax.sharding import PartitionSpec as P


def tile_terms(row_x, row_left, col_x, col_right, inv_scale):
    col_scaled = col_x * inv_scale
    row_sq = jnp.sum(row_x * inv_scale * row_x, axis=1)
    col_sq = jnp.sum(col_scaled * col_x, axis=1)
    contract_last = (((1,), (1,)), ((), ()))
    inner_prod = lax.dot_general(
        row_x,
        col_scaled,
        contract_last,
        precision=lax.Precision.HIGHEST,
        preferred_element_type=jnp.float32,
    )
    mixing = lax.dot_general(
        row_left,
        col_right,
        contract_last,
        precision=lax.Precision.HIGHEST,
        preferred_element_type=jnp.float32,
    )
    coupling = mixing * jnp.exp(-0.5 * (row_sq[:, None] + col_sq[None, :] - 2.0 * inner_prod))
    row_pull = jnp.dot(
        coupling, col_x, precision=lax.Precision.HIGHEST, preferred_element_type=jnp.float32
    )
    col_pull = lax.dot_general(
        coupling,
        row_x,
        (((0,), (0,)), ((), ())),
        precision=lax.Precision.HIGHEST,
        preferred_element_type=jnp.float32,
    )
    row_term = (row_pull - jnp.sum(coupling, axis=1)[:, None] * row_x) * inv_scale
    col_term = (col_pull - jnp.sum(coupling, axis=0)[:, None] * col_x) * inv_scale
    return (row_term, col_term)


def on_device(features, inv_scale, probe_u, solve_v):
    row_x, row_u = (
        lax.all_gather(features, "col", axis=0, tiled=True),
        lax.all_gather(probe_u, "col", axis=0, tiled=True),
    )
    col_x, col_v = (
        lax.all_gather(features, "row", axis=0, tiled=True),
        lax.all_gather(solve_v, "row", axis=0, tiled=True),
    )
    row_acc, col_acc = tile_terms(row_x, row_u, col_x, col_v, inv_scale)
    row_own = lax.psum_scatter(row_acc, "col", scatter_dimension=0, tiled=True)
    col_own = lax.psum_scatter(col_acc, "row", scatter_dimension=0, tiled=True)
    return row_own + col_own


def solution(mesh):
    return jax.shard_map(
        on_device,
        mesh=mesh,
        in_specs=(P(("row", "col"), None), P(), P(("row", "col"), None), P(("row", "col"), None)),
        out_specs=P(("row", "col"), None),
        check_vma=False,
    )
```

profile of v0, /device:TPU:0, one launch (start us, length us, event | category | flops | bytes accessed | tf_op | source)
XLA Modules:
  0.0 121.0 jit_solution(7620445535280970411)
XLA Ops:
  6.5 0.0 copy-start
  6.5 0.0 reduce-scatter.3.cloned.1.call-start
  6.5 15.8 %all_gather.14 = f32[192,256]{1,0:T(8,128)S(1)} all-gather(f32[48,256]{1,0:T(8,128)} %param.4), channel_id=1, replica_groups=mesh['row'=8,'col'=4] {'col'}, dimensions={0}, use_global_device_ids=true | all-gather | bytes 245760 | tf_op jit(solution)/shard_map/all_gather | solution.py:44
  22.3 0.0 copy-done
  22.3 0.0 copy-start.3
  22.3 9.7 %all_gather.15 = f32[384,256]{1,0:T(8,128)S(1)} all-gather(f32[48,256]{1,0:T(8,128)S(1)} %copy-done), channel_id=1, replica_groups=mesh['row'=8,'col'=4] {'row'}, dimensions={0}, use_global_device_ids=true | all-gather | bytes 442368 | tf_op jit(solution)/shard_map/all_gather | solution.py:48
  32.0 0.0 copy-done.3
  32.0 0.0 copy-start.2
  32.0 13.5 %all_gather.12 = f32[192,64]{1,0:T(8,128)S(1)} all-gather(f32[48,64]{1,0:T(8,128)S(1)} %copy-done.3), channel_id=1, replica_groups=mesh['row'=8,'col'=4] {'col'}, dimensions={0}, use_global_device_ids=true | all-gather | bytes 61440 | tf_op jit(solution)/shard_map/all_gather | solution.py:45
  45.5 0.0 copy-done.2
  45.5 0.0 copy-start.1
  45.5 9.4 %all_gather.13 = f32[384,64]{1,0:T(8,128)S(1)} all-gather(f32[48,64]{1,0:T(8,128)S(1)} %copy-done.2), channel_id=1, replica_groups=mesh['row'=8,'col'=4] {'row'}, dimensions={0}, use_global_device_ids=true | all-gather | bytes 110592 | tf_op jit(solution)/shard_map/all_gather | solution.py:49
  54.9 0.0 copy-done.1
  54.9 0.1 fusion.8
  55.0 0.1 fusion.7
  55.1 0.6 fusion.4
  55.7 0.5 fusion.10
  56.3 1.2 fusion.5
  57.4 0.0 reduce-scatter.3.cloned.1.call-update
  57.5 0.0 reduce-scatter.5.cloned.1.call-start
  57.5 1.6 %fusion = f32[384,256]{1,0:T(8,128)} fusion(f32[192,384]{1,0:T(8,128)S(1)} %get-tuple-element.7, f32[192,256]{1,0:T(8,128)S(1)} %all_gather.14, f32[384,256]{1,0:T(8,128)S(1)} %all_gather.15, f32[384]{0:T(512)S(1)} %get-tuple-element.5, f32[256]{0:T(256)S(1)} %copy-done.1), kind=kOutput, calls=%fused_computation.1 | convolution fusion | flops 226787328 | bytes 1280512 | tf_op jit(solution)/shard_map/dot_general | solution.py:30
  59.1 0.0 reduce-scatter.5.cloned.1.call-update
  59.1 18.2 %reduce-scatter.3.cloned.1.call-done = f32[48,256]{1,0:T(8,128)} async-done(((f32[192,256]{1,0:T(8,128)}), f32[48,256]{1,0:T(8,128)}) %reduce-scatter.3.cloned.1.call-update) | async-done | bytes 49168 | tf_op jit(solution)/shard_map/reduce_scatter | solution.py:52
  77.3 35.4 %reduce-scatter.5.cloned.1.call-done = f32[48,256]{1,0:T(8,128)} async-done(((f32[384,256]{1,0:T(8,128)}), f32[48,256]{1,0:T(8,128)}) %reduce-scatter.5.cloned.1.call-update) | async-done | bytes 49168 | tf_op jit(solution)/shard_map/reduce_scatter | solution.py:53
  112.7 1.4 %add.23 = f32[48,256]{1,0:T(8,128)} add(f32[48,256]{1,0:T(8,128)} %reduce-scatter.3.cloned.1.call-done, f32[48,256]{1,0:T(8,128)} %reduce-scatter.5.cloned.1.call-done) | non-fusion elementwise | flops 12288 | bytes 147456 | tf_op jit(solution)/shard_map/add | solution.py:54
Async XLA Ops:
  6.5 15.8 %copy-start = (f32[48,256]{1,0:T(8,128)S(1)}, f32[48,256]{1,0:T(8,128)}, u32[]{:S(2)}) copy-start(f32[48,256]{1,0:T(8,128)} %param.4) | copy-start | bytes 147460
  6.5 70.7 %reduce-scatter.3.cloned.1.call-start = ((), (), s32[]{:S(2)}) async-start(), calls=%async_computation.2 | async-start | bytes 245760 | tf_op jit(solution)/shard_map/reduce_scatter | solution.py:52
  22.3 9.7 %copy-start.3 = (f32[48,64]{1,0:T(8,128)S(1)}, f32[48,64]{1,0:T(8,128)}, u32[]{:S(2)}) copy-start(f32[48,64]{1,0:T(8,128)} %param.6) | copy-start | bytes 36868
  32.0 13.5 %copy-start.2 = (f32[48,64]{1,0:T(8,128)S(1)}, f32[48,64]{1,0:T(8,128)}, u32[]{:S(2)}) copy-start(f32[48,64]{1,0:T(8,128)} %param.7) | copy-start | bytes 36868
  45.5 9.4 %copy-start.1 = (f32[256]{0:T(256)S(1)}, f32[256]{0:T(256)}, u32[]{:S(2)}) copy-start(f32[256]{0:T(256)} %param.5) | copy-start | bytes 3076
  57.5 55.2 %reduce-scatter.5.cloned.1.call-start = ((), (), s32[]{:S(2)}) async-start(), calls=%async_computation.3 | async-start | bytes 442368 | tf_op jit(solution)/shard_map/reduce_scatter | solution.py:53
Sparse Core Ops, SparseCore 0:
  57.6 19.6 reduce-scatter.2
  80.6 32.0 reduce-scatter.4
where the time goes:
time: 121 us
  waiting for transfers between devices  53.6 us (44%)
  blocking collectives  48.3 us (40%)
  between operations  13.4 us (11%)
  matrix products  3.86 us (3%)
  other arithmetic  1.71 us (1%)
    reduce_scatter x1, waiting for transfers between devices, on_device(): col_own = lax.psum_scatter(col_acc, 'row', scatter_dimension=0, tiled=True)  35.4 us
    reduce_scatter x1, waiting for transfers between devices, on_device(): row_own = lax.psum_scatter(row_acc, 'col', scatter_dimension=0, tiled=True)  18.2 us
    all_gather x1, blocking collectives, on_device(): lax.all_gather(features, 'col', axis=0, tiled=True)  15.8 us
    all_gather x1, blocking collectives, on_device(): lax.all_gather(probe_u, 'col', axis=0, tiled=True)  13.5 us
    all_gather x1, blocking collectives, on_device(): lax.all_gather(features, 'row', axis=0, tiled=True)  9.71 us
    all_gather x1, blocking collectives, on_device(): lax.all_gather(solve_v, 'row', axis=0, tiled=True)  9.37 us
  transfers between devices with their start and end apart: 2, of which 2 were waited for; matrix products, arithmetic and copies ran while one was open for 1% of the time, Pallas kernels for 0%

commit v1 on v0

v1 whole, which is shorter than its diff:
```python
import functools
import math

import jax
import jax.numpy as jnp
from jax import lax
from jax.experimental import pallas as pl
from jax.experimental.pallas import tpu as pltpu
from jax.sharding import PartitionSpec as P

MESH = pl.DeviceIdType.MESH
LAST = (((1,), (1,)), ((), ()))


def split(count):
    return max(part for part in range(1, math.isqrt(count) + 1) if count % part == 0)


def exact_dot(left, right, dims):
    return lax.dot_general(
        left, right, dims, precision=lax.Precision.HIGHEST, preferred_element_type=jnp.float32
    )


def kernel(
    sizes,
    x_ref,
    scale_ref,
    u_ref,
    v_ref,
    out_ref,
    row_buf,
    col_buf,
    part,
    landed,
    scale_buf,
    u_buf,
    v_buf,
    local_sem,
    row_send,
    row_recv,
    col_send,
    col_recv,
    twin_send,
    twin_recv,
    red_send,
    red_recv,
):
    n_core, n_a, n_b, n_c, n_d = sizes
    points, width = x_ref.shape
    rank = u_ref.shape[1]
    row, col = lax.axis_index("row"), lax.axis_index("col")
    core, chip = lax.rem(row, n_core), lax.div(row, n_core)
    a, c = lax.rem(chip, n_a), lax.div(chip, n_a)
    b, d = lax.rem(col, n_b), lax.div(col, n_b)

    def device(da=0, db=0, dc=0, dd=0, dcore=0):
        to_chip = lax.rem(c + dc, n_c) * n_a + lax.rem(a + da, n_a)
        to_row = to_chip * n_core + lax.rem(core + dcore, n_core)
        return (to_row, lax.rem(d + dd, n_d) * n_b + lax.rem(b + db, n_b))

    def row_slot(da, db):
        return da * n_b + db

    def col_slot(dc, dd):
        return dc * n_d + dd

    n_row, n_col = n_a * n_b, n_c * n_d
    peers = [device(da=i, db=j) for i in range(n_a) for j in range(n_b) if i + j > 0]
    peers += [device(dc=i) for i in range(1, n_c)]
    peers += [device(dd=i) for i in range(1, n_d)]
    peers += [device(dcore=i) for i in range(1, n_core)]
    barrier = pltpu.get_barrier_semaphore()
    for peer in peers:
        pl.semaphore_signal(barrier, inc=1, device_id=peer, device_id_type=MESH)

    loads = [
        pltpu.make_async_copy(x_ref, row_buf.at[0, :, pl.ds(0, width)], local_sem.at[0]),
        pltpu.make_async_copy(u_ref, u_buf, local_sem.at[1]),
        pltpu.make_async_copy(v_ref, v_buf, local_sem.at[2]),
        pltpu.make_async_copy(scale_ref, scale_buf, local_sem.at[3]),
    ]
    for load in loads:
        load.start()
    for load in loads:
        load.wait()
    row_buf[0, :, width:] = jnp.concatenate([u_buf[...], v_buf[...]], axis=1)
    col_buf[0] = row_buf[0]
    pl.semaphore_wait(barrier, len(peers))

    def remote(src, dst, send, recv, to):
        return pltpu.make_async_remote_copy(
            src_ref=src, dst_ref=dst, send_sem=send, recv_sem=recv, device_id=to, device_id_type=MESH
        )

    def row_copy(src, dst, **step):
        back = {name: {"da": n_a, "db": n_b}[name] - by for name, by in step.items()}
        return remote(
            row_buf.at[src], row_buf.at[dst], row_send.at[dst], row_recv.at[dst], device(**back)
        )

    def col_copy(src, dst, **step):
        back = {name: {"dc": n_c, "dd": n_d}[name] - by for name, by in step.items()}
        return remote(
            col_buf.at[src], col_buf.at[dst], col_send.at[dst], col_recv.at[dst], device(**back)
        )

    def twin_copy(slot):
        return remote(
            col_buf.at[slot],
            col_buf.at[n_col + slot],
            twin_send.at[slot],
            twin_recv.at[slot],
            device(dcore=1),
        )

    near = [row_copy(0, row_slot(0, j), db=j) for j in range(1, n_b)]
    far = [col_copy(0, col_slot(0, j), dd=j) for j in range(1, n_d)]
    side = [
        [row_copy(row_slot(0, j), row_slot(i, j), da=i) for i in range(1, n_a)] for j in range(n_b)
    ]
    over = [
        [col_copy(col_slot(0, j), col_slot(i, j), dc=i) for i in range(1, n_c)] for j in range(n_d)
    ]
    twin = [twin_copy(slot) for slot in range(n_col)] if n_core > 1 else []

    def start(copies):
        for copy in copies:
            copy.start()

    start(far)
    start(near)
    start(over[0])
    start(side[0])
    start(twin[:1])
    for j, copy in enumerate(near, 1):
        copy.wait_recv()
        start(side[j])
    for j, copy in enumerate(far, 1):
        copy.wait_recv()
        start(over[j])
        start(twin[j : j + 1])
    for j in range(n_d):
        for i, copy in enumerate(over[j], 1):
            copy.wait_recv()
            start(twin[col_slot(i, j) : col_slot(i, j) + 1])
    for copies in side:
        for copy in copies:
            copy.wait_recv()
    for copy in twin:
        copy.wait_recv()

    scale = scale_buf[...].reshape(1, width)
    cols = col_buf[...].reshape(n_core * n_col * points, width + 2 * rank)
    col_x, col_uv = cols[:, :width], cols[:, width:]
    col_scaled = col_x * scale
    col_sq = exact_dot(jnp.ones((8, width), jnp.float32), col_scaled * col_x, LAST)[:1]
    reduces = []

    def tile(first, last):
        rows = row_buf[first:last].reshape((last - first) * points, width + 2 * rank)
        row_x, row_uv = rows[:, :width], rows[:, width:]
        row_vu = jnp.concatenate([row_uv[:, rank:], row_uv[:, :rank]], axis=1)
        row_sq = jnp.sum(row_x * scale * row_x, axis=1, keepdims=True)
        inner = exact_dot(row_x, col_scaled, LAST)
        mixing = exact_dot(row_vu, col_uv, LAST)
        coupling = mixing * jnp.exp(-0.5 * (row_sq + col_sq - 2.0 * inner))
        pulled = exact_dot(coupling, col_x, (((1,), (0,)), ((), ())))
        term = pulled - jnp.sum(coupling, axis=1, keepdims=True) * row_x
        part[first:last] = term.reshape(last - first, points, width)

    if n_row > 1:
        step = 3
        for first in range(1, n_row, step):
            tile(first, min(first + step, n_row))
            for slot in range(first, min(first + step, n_row)):
                i, j = slot // n_b, slot % n_b
                copy = remote(
                    part.at[slot],
                    landed.at[slot],
                    red_send.at[slot],
                    red_recv.at[slot],
                    device(da=i, db=j),
                )
                copy.start()
                reduces.append(copy)
    tile(0, 1)
    total = part[0]
    for slot, copy in enumerate(reduces, 1):
        copy.wait_recv()
        total = total + landed[slot]
    out_ref[...] = total * scale

    for copies in (near, far, *side, *over, twin, reduces):
        for copy in copies:
            copy.wait_send()


def on_device(sizes, features, inv_scale, probe_u, solve_v):
    n_core, n_a, n_b, n_c, n_d = sizes
    points, width = features.shape
    rank = probe_u.shape[1]
    n_row, n_col = n_a * n_b, n_c * n_d
    f32, dma = jnp.float32, pltpu.SemaphoreType.DMA
    return pl.pallas_call(
        functools.partial(kernel, sizes),
        out_shape=jax.ShapeDtypeStruct((points, width), f32),
        in_specs=[pl.BlockSpec(memory_space=pl.ANY)] * 4,
        out_specs=pl.BlockSpec(memory_space=pltpu.VMEM),
        scratch_shapes=[
            pltpu.VMEM((n_row, points, width + 2 * rank), f32),
            pltpu.VMEM((n_core * n_col, points, width + 2 * rank), f32),
            pltpu.VMEM((n_row, points, width), f32),
            pltpu.VMEM((n_row, points, width), f32),
            pltpu.VMEM((width,), f32),
            pltpu.VMEM((points, rank), f32),
            pltpu.VMEM((points, rank), f32),
            dma((4,)),
            dma((n_row,)),
            dma((n_row,)),
            dma((n_col,)),
            dma((n_col,)),
            dma((n_col,)),
            dma((n_col,)),
            dma((n_row,)),
            dma((n_row,)),
        ],
        compiler_params=pltpu.CompilerParams(
            collective_id=0, has_side_effects=True, vmem_limit_bytes=48 * 2**20
        ),
    )(features, inv_scale, probe_u, solve_v)


def solution(mesh):
    rows, cols = mesh.shape["row"], mesh.shape["col"]
    n_core = 2 if rows % 2 == 0 else 1
    chips = rows // n_core
    n_a, n_b = split(chips), split(cols)
    sizes = (n_core, n_a, n_b, chips // n_a, cols // n_b)
    return jax.shard_map(
        functools.partial(on_device, sizes),
        mesh=mesh,
        in_specs=(P(("row", "col"), None), P(), P(("row", "col"), None), P(("row", "col"), None)),
        out_specs=P(("row", "col"), None),
        check_vma=False,
    )
```

time: 121 us -> 23.4 us (0.19)
  waiting for transfers between devices: 53.6 us -> 0 us
  blocking collectives: 48.3 us -> 0 us
  Pallas kernels: 0 us -> 19.5 us
  between operations: 13.4 us -> 0.01 us
  matrix products: 3.86 us -> 0 us
  local copies, waits for them, and re-layouts: 0.01 us -> 3.57 us
  other arithmetic: 1.71 us -> 0 us
    reduce_scatter x2 -> x0, waiting for transfers between devices: 53.6 us -> none  [the longest x1 35.4 us: on_device(): col_own = lax.psum_scatter(col_acc, 'row', scatter_dimension=0, tiled=True)]
    all_gather x4 -> x0, blocking collectives: 48.3 us -> none  [the longest x1 15.8 us: on_device(): lax.all_gather(features, 'col', axis=0, tiled=True)]
    pallas_call x0 -> x1, Pallas kernels: none -> 19.5 us  [on_device(): pl.pallas_call(functools.partial(kernel, sizes), out_shape=jax.ShapeDtype...]
    dot_general x4 -> x0, matrix products: 3.86 us -> none  [the longest x1 1.57 us: tile_terms(): lax.dot_general(coupling, row_x, (((0,), (0,)), ((), ())), precision=lax....]
    unnamed x8 -> x9, local copies, waits for them, and re-layouts: 0.01 us -> 3.57 us
    add x1 -> x0, other arithmetic: 1.45 us -> none  [on_device(): return row_own + col_own]
  transfers between devices with their start and end apart: 2 -> 0, of which waited for: 2 -> 0; matrix products, arithmetic and copies ran while one was open for 1% -> 0% of each run, Pallas kernels for 0% -> 0%
where the time goes in v1:
time: 23.4 us; the launch traced here: 23.1 us
  Pallas kernels  19.5 us (83%)
  local copies, waits for them, and re-layouts  3.57 us (15%)
    pallas_call x1, Pallas kernels, on_device(): pl.pallas_call(functools.partial(kernel, sizes), out_shape=jax.ShapeDtype...  19.5 us
    unnamed x9, local copies, waits for them, and re-layouts  3.57 us

profile of v1, /device:TPU:0, one launch (start us, length us, event | category | flops | bytes accessed | tf_op | source)
XLA Modules:
  0.0 23.1 jit_solution(15972902055666767078)
XLA Ops:
  0.0 0.0 copy-start
  0.0 0.8 %copy-done = f32[48,256]{1,0:T(8,128)S(1)} copy-done((f32[48,256]{1,0:T(8,128)S(1)}, f32[48,256]{1,0:T(8,128)}, u32[]{:S(2)}) %copy-start) | copy-done | bytes 49176
  0.8 0.0 copy-start.1
  0.8 0.7 %copy-done.1 = f32[48,64]{1,0:T(8,128)S(1)} copy-done((f32[48,64]{1,0:T(8,128)S(1)}, f32[48,64]{1,0:T(8,128)}, u32[]{:S(2)}) %copy-start.1) | copy-done | bytes 12312
  1.5 0.0 copy-start.2
  1.5 0.7 %copy-done.2 = f32[48,64]{1,0:T(8,128)S(1)} copy-done((f32[48,64]{1,0:T(8,128)S(1)}, f32[48,64]{1,0:T(8,128)}, u32[]{:S(2)}) %copy-start.2) | copy-done | bytes 12312
  2.3 0.0 copy-start.3
  2.3 0.7 %copy-done.3 = f32[256]{0:T(256)S(1)} copy-done((f32[256]{0:T(256)S(1)}, f32[256]{0:T(256)}, u32[]{:S(2)}) %copy-start.3) | copy-done | bytes 1048
  3.0 19.5 %shard_map.46 = f32[48,256]{1,0:T(8,128)S(1)} custom-call(f32[48,256]{1,0:T(8,128)S(1)} %copy-done, f32[256]{0:T(256)S(1)} %copy-done.3, f32[48,64]{1,0:T(8,128)S(1)} %copy-done.1, f32[48,64]{1,0:T(8,128)S(1)} %copy-done.2), custom_call_target="tpu_custom_call" | custom-call | tf_op jit(solution)/shard_map/pallas_call | solution.py:205
  22.5 0.6 %copy.6 = f32[48,256]{1,0:T(8,128)} copy(f32[48,256]{1,0:T(8,128)S(1)} %shard_map.46) | data formatting | bytes 98304
Async XLA Ops:
  0.0 0.8 %copy-start = (f32[48,256]{1,0:T(8,128)S(1)}, f32[48,256]{1,0:T(8,128)}, u32[]{:S(2)}) copy-start(f32[48,256]{1,0:T(8,128)} %x_ref.1) | copy-start | bytes 147460
  0.8 0.7 %copy-start.1 = (f32[48,64]{1,0:T(8,128)S(1)}, f32[48,64]{1,0:T(8,128)}, u32[]{:S(2)}) copy-start(f32[48,64]{1,0:T(8,128)} %u_ref.1) | copy-start | bytes 36868
  1.5 0.7 %copy-start.2 = (f32[48,64]{1,0:T(8,128)S(1)}, f32[48,64]{1,0:T(8,128)}, u32[]{:S(2)}) copy-start(f32[48,64]{1,0:T(8,128)} %v_ref.1) | copy-start | bytes 36868
  2.3 0.7 %copy-start.3 = (f32[256]{0:T(256)S(1)}, f32[256]{0:T(256)}, u32[]{:S(2)}) copy-start(f32[256]{0:T(256)} %scale_ref.1) | copy-start | bytes 3076

commit v2 on v1

--- a/solution.py
+++ b/solution.py
@@ -10,16 +10,30 @@
 
 MESH = pl.DeviceIdType.MESH
 LAST = (((1,), (1,)), ((), ()))
+FIRST = (((1,), (0,)), ((), ()))
 
 
 def split(count):
     return max(part for part in range(1, math.isqrt(count) + 1) if count % part == 0)
 
 
-def exact_dot(left, right, dims):
-    return lax.dot_general(
-        left, right, dims, precision=lax.Precision.HIGHEST, preferred_element_type=jnp.float32
-    )
+def dot(left, right, dims):
+    return lax.dot_general(left, right, dims, preferred_element_type=jnp.float32)
+
+
+def halves(value):
+    hi = value.astype(jnp.bfloat16)
+    return hi, (value - hi.astype(jnp.float32)).astype(jnp.bfloat16)
+
+
+def ends(square, side):
+    lane = lax.broadcasted_iota(jnp.int32, (square.shape[0], 128), 1)
+    rest, lanes = -0.5 * square, jnp.where(lane < 6, 1.0, 0.0)
+    for index in range(3):
+        piece = rest.astype(jnp.bfloat16).astype(jnp.float32)
+        lanes = jnp.where(lane == 3 * side + index, piece, lanes)
+        rest = rest - piece
+    return lanes.astype(jnp.bfloat16)
 
 
 def kernel(
@@ -147,45 +161,61 @@
     for copies in side:
         for copy in copies:
             copy.wait_recv()
+
+    scale = scale_buf[...].reshape(1, width)
+    rows = row_buf[...].reshape(n_row * points, width + 2 * rank)
+    row_x, row_uv = rows[:, :width], rows[:, width:]
+    row_sq = jnp.sum(row_x * scale * row_x, axis=1, keepdims=True)
+    row_x_hi, row_x_lo = halves(row_x)
+    row_left = jnp.concatenate([row_x_hi, row_x_lo, row_x_hi, ends(row_sq, 1)], axis=1)
+    vu_hi, vu_lo = halves(jnp.concatenate([row_uv[:, rank:], row_uv[:, :rank]], axis=1))
+    vu_left = jnp.concatenate([vu_hi, vu_lo, vu_hi], axis=1)
+
+    def chunk(core_slot):
+        cols = col_buf[core_slot * n_col : (core_slot + 1) * n_col]
+        cols = cols.reshape(n_col * points, width + 2 * rank)
+        col_x = cols[:, :width]
+        col_scaled = col_x * scale
+        col_sq = jnp.sum(col_scaled * col_x, axis=1, keepdims=True)
+        scaled_hi, scaled_lo = halves(col_scaled)
+        col_right = jnp.concatenate([scaled_hi, scaled_hi, scaled_lo, ends(col_sq, 0)], axis=1)
+        uv_hi, uv_lo = halves(cols[:, width:])
+        uv_right = jnp.concatenate([uv_hi, uv_hi, uv_lo], axis=1)
+        coupling = dot(vu_left, uv_right, LAST) * jnp.exp(dot(row_left, col_right, LAST))
+        hi, lo = halves(coupling)
+        col_x_hi, col_x_lo = halves(col_x)
+        both = dot(jnp.concatenate([hi, lo], axis=0), col_x_hi, FIRST)
+        pulled = both[: n_row * points] + both[n_row * points :] + dot(hi, col_x_lo, FIRST)
+        return coupling, pulled, jnp.sum(coupling, axis=1, keepdims=True)
+
+    coupling, pulled, sums = chunk(0)
+    place = [lax.broadcasted_iota(jnp.int32, (points, n_col * points), axis) for axis in (0, 1)]
+    diagonal = jnp.where(place[0] == place[1], coupling[:points], 0.0)
+    diagonal = jnp.sum(diagonal, axis=1, keepdims=True)
+    diag_hi, diag_lo = (half.astype(jnp.float32) for half in halves(diagonal))
+    own = row_x[:points]
+    own_hi, own_lo = (half.astype(jnp.float32) for half in halves(own))
+    rest = diagonal * own - diag_hi * own_hi - diag_hi * own_lo - diag_lo * own_hi
+
     for copy in twin:
         copy.wait_recv()
-
-    scale = scale_buf[...].reshape(1, width)
-    cols = col_buf[...].reshape(n_core * n_col * points, width + 2 * rank)
-    col_x, col_uv = cols[:, :width], cols[:, width:]
-    col_scaled = col_x * scale
-    col_sq = exact_dot(jnp.ones((8, width), jnp.float32), col_scaled * col_x, LAST)[:1]
+    for core_slot in range(1, n_core):
+        _, more_pulled, more_sums = chunk(core_slot)
+        pulled, sums = pulled + more_pulled, sums + more_sums
+    part[...] = (pulled - sums * row_x).reshape(n_row, points, width)
+
     reduces = []
-
-    def tile(first, last):
-        rows = row_buf[first:last].reshape((last - first) * points, width + 2 * rank)
-        row_x, row_uv = rows[:, :width], rows[:, width:]
-        row_vu = jnp.concatenate([row_uv[:, rank:], row_uv[:, :rank]], axis=1)
-        row_sq = jnp.sum(row_x * scale * row_x, axis=1, keepdims=True)
-        inner = exact_dot(row_x, col_scaled, LAST)
-        mixing = exact_dot(row_vu, col_uv, LAST)
-        coupling = mixing * jnp.exp(-0.5 * (row_sq + col_sq - 2.0 * inner))
-        pulled = exact_dot(coupling, col_x, (((1,), (0,)), ((), ())))
-        term = pulled - jnp.sum(coupling, axis=1, keepdims=True) * row_x
-        part[first:last] = term.reshape(last - first, points, width)
-
-    if n_row > 1:
-        step = 3
-        for first in range(1, n_row, step):
-            tile(first, min(first + step, n_row))
-            for slot in range(first, min(first + step, n_row)):
-                i, j = slot // n_b, slot % n_b
-                copy = remote(
-                    part.at[slot],
-                    landed.at[slot],
-                    red_send.at[slot],
-                    red_recv.at[slot],
-                    device(da=i, db=j),
-                )
-                copy.start()
-                reduces.append(copy)
-    tile(0, 1)
-    total = part[0]
+    for slot in range(1, n_row):
+        copy = remote(
+            part.at[slot],
+            landed.at[slot],
+            red_send.at[slot],
+            red_recv.at[slot],
+            device(da=slot // n_b, db=slot % n_b),
+        )
+        copy.start()
+        reduces.append(copy)
+    total = part[0] + rest
     for slot, copy in enumerate(reduces, 1):
         copy.wait_recv()
         total = total + landed[slot]
@@ -205,7 +235,7 @@
     return pl.pallas_call(
         functools.partial(kernel, sizes),
         out_shape=jax.ShapeDtypeStruct((points, width), f32),
-        in_specs=[pl.BlockSpec(memory_space=pl.ANY)] * 4,
+        in_specs=[pl.BlockSpec(memory_space=pltpu.HBM)] * 4,
         out_specs=pl.BlockSpec(memory_space=pltpu.VMEM),
         scratch_shapes=[
             pltpu.VMEM((n_row, points, width + 2 * rank), f32),
@@ -226,7 +256,7 @@
             dma((n_row,)),
         ],
         compiler_params=pltpu.CompilerParams(
-            collective_id=0, has_side_effects=True, vmem_limit_bytes=48 * 2**20
+            collective_id=0, has_side_effects=True, vmem_limit_bytes=60 * 2**20
         ),
     )(features, inv_scale, probe_u, solve_v)
 

time: 23.4 us -> 22 us (0.940)
  local copies, waits for them, and re-layouts: 3.57 us -> 1.42 us
  Pallas kernels: 19.5 us -> 20.3 us
    unnamed x9 -> x1, local copies, waits for them, and re-layouts: 3.57 us -> 1.42 us
    pallas_call x1, Pallas kernels: 19.5 us -> 20.3 us  [on_device(): pl.pallas_call(functools.partial(kernel, sizes), out_shape=jax.ShapeDtype...]
where the time goes in v2:
time: 22 us; the launch traced here: 21.8 us
  Pallas kernels  20.3 us (92%)
  local copies, waits for them, and re-layouts  1.42 us (6%)
    pallas_call x1, Pallas kernels, on_device(): pl.pallas_call(functools.partial(kernel, sizes), out_shape=jax.ShapeDtype...  20.3 us
    unnamed x1, local copies, waits for them, and re-layouts  1.42 us

profile of v2, /device:TPU:0, one launch (start us, length us, event | category | flops | bytes accessed | tf_op | source)
XLA Modules:
  0.0 21.8 jit_solution(2019943844723486286)
XLA Ops:
  0.0 20.3 %shard_map.46 = f32[48,256]{1,0:T(8,128)} custom-call(f32[48,256]{1,0:T(8,128)} %x_ref.1, f32[256]{0:T(256)} %scale_ref.1, f32[48,64]{1,0:T(8,128)} %u_ref.1, f32[48,64]{1,0:T(8,128)} %v_ref.1), custom_call_target="tpu_custom_call" | custom-call | tf_op jit(solution)/shard_map/pallas_call | solution.py:235
  20.3 1.4 %copy.6 = f32[48,256]{1,0:T(8,128)} copy(f32[48,256]{1,0:T(8,128)} %shard_map.46) | data formatting | bytes 98304

commit v3 on v2

--- a/solution.py
+++ b/solution.py
@@ -38,19 +38,13 @@
 
 def kernel(
     sizes,
-    x_ref,
+    block_ref,
     scale_ref,
-    u_ref,
-    v_ref,
     out_ref,
     row_buf,
     col_buf,
     part,
     landed,
-    scale_buf,
-    u_buf,
-    v_buf,
-    local_sem,
     row_send,
     row_recv,
     col_send,
@@ -61,8 +55,8 @@
     red_recv,
 ):
     n_core, n_a, n_b, n_c, n_d = sizes
-    points, width = x_ref.shape
-    rank = u_ref.shape[1]
+    points, width = out_ref.shape
+    rank = (block_ref.shape[1] - width) // 2
     row, col = lax.axis_index("row"), lax.axis_index("col")
     core, chip = lax.rem(row, n_core), lax.div(row, n_core)
     a, c = lax.rem(chip, n_a), lax.div(chip, n_a)
@@ -88,18 +82,8 @@
     for peer in peers:
         pl.semaphore_signal(barrier, inc=1, device_id=peer, device_id_type=MESH)
 
-    loads = [
-        pltpu.make_async_copy(x_ref, row_buf.at[0, :, pl.ds(0, width)], local_sem.at[0]),
-        pltpu.make_async_copy(u_ref, u_buf, local_sem.at[1]),
-        pltpu.make_async_copy(v_ref, v_buf, local_sem.at[2]),
-        pltpu.make_async_copy(scale_ref, scale_buf, local_sem.at[3]),
-    ]
-    for load in loads:
-        load.start()
-    for load in loads:
-        load.wait()
-    row_buf[0, :, width:] = jnp.concatenate([u_buf[...], v_buf[...]], axis=1)
-    col_buf[0] = row_buf[0]
+    row_buf[0] = block_ref[...]
+    col_buf[0] = block_ref[...]
     pl.semaphore_wait(barrier, len(peers))
 
     def remote(src, dst, send, recv, to):
@@ -162,7 +146,7 @@
         for copy in copies:
             copy.wait_recv()
 
-    scale = scale_buf[...].reshape(1, width)
+    scale = scale_ref[...].reshape(1, width)
     rows = row_buf[...].reshape(n_row * points, width + 2 * rank)
     row_x, row_uv = rows[:, :width], rows[:, width:]
     row_sq = jnp.sum(row_x * scale * row_x, axis=1, keepdims=True)
@@ -235,17 +219,13 @@
     return pl.pallas_call(
         functools.partial(kernel, sizes),
         out_shape=jax.ShapeDtypeStruct((points, width), f32),
-        in_specs=[pl.BlockSpec(memory_space=pltpu.HBM)] * 4,
+        in_specs=[pl.BlockSpec(memory_space=pltpu.VMEM)] * 2,
         out_specs=pl.BlockSpec(memory_space=pltpu.VMEM),
         scratch_shapes=[
             pltpu.VMEM((n_row, points, width + 2 * rank), f32),
             pltpu.VMEM((n_core * n_col, points, width + 2 * rank), f32),
             pltpu.VMEM((n_row, points, width), f32),
             pltpu.VMEM((n_row, points, width), f32),
-            pltpu.VMEM((width,), f32),
-            pltpu.VMEM((points, rank), f32),
-            pltpu.VMEM((points, rank), f32),
-            dma((4,)),
             dma((n_row,)),
             dma((n_row,)),
             dma((n_col,)),
@@ -256,9 +236,9 @@
             dma((n_row,)),
         ],
         compiler_params=pltpu.CompilerParams(
-            collective_id=0, has_side_effects=True, vmem_limit_bytes=60 * 2**20
+            collective_id=0, has_side_effects=True, vmem_limit_bytes=48 * 2**20
         ),
-    )(features, inv_scale, probe_u, solve_v)
+    )(jnp.concatenate([features, probe_u, solve_v], axis=1), inv_scale)
 
 
 def solution(mesh):

time: 22 us -> 21.4 us (0.973)
  other arithmetic: 0 us -> 0.92 us
  local copies, waits for them, and re-layouts: 1.42 us -> 0.63 us
  Pallas kernels: 20.3 us -> 19.7 us
    concatenate x0 -> x1, other arithmetic: none -> 0.92 us  [on_device(): jnp.concatenate([features, probe_u, solve_v], axis=1)]
    unnamed x1 -> x3, local copies, waits for them, and re-layouts: 1.42 us -> 0.63 us
    pallas_call x1, Pallas kernels: 20.3 us -> 19.7 us  [on_device(): pl.pallas_call(functools.partial(kernel, sizes), out_shape=jax.ShapeDtype...]
where the time goes in v3:
time: 21.4 us; the launch traced here: 21.3 us
  Pallas kernels  19.7 us (92%)
  other arithmetic  0.92 us (4%)
  local copies, waits for them, and re-layouts  0.63 us (3%)
    pallas_call x1, Pallas kernels, on_device(): pl.pallas_call(functools.partial(kernel, sizes), out_shape=jax.ShapeDtype...  19.7 us
    concatenate x1, other arithmetic, on_device(): jnp.concatenate([features, probe_u, solve_v], axis=1)  0.92 us
    unnamed x3, local copies, waits for them, and re-layouts  0.63 us

profile of v3, /device:TPU:0, one launch (start us, length us, event | category | flops | bytes accessed | tf_op | source)
XLA Modules:
  0.0 21.3 jit_solution(14007254923136556292)
XLA Ops:
  0.0 0.0 copy-start
  0.0 0.9 %pad_maximum_fusion.block_ref = f32[48,384]{1,0:T(8,128)S(1)} fusion(f32[48,64]{1,0:T(8,128)} %param.7, f32[48,64]{1,0:T(8,128)} %param.6, f32[48,256]{1,0:T(8,128)} %param.4), kind=kLoop, calls=%fused_computation | loop fusion | flops 36864 | bytes 147456 | tf_op jit(solution)/shard_map/concatenate | solution.py:241
  0.9 0.0 copy-done
  0.9 19.7 %shard_map.46 = f32[48,256]{1,0:T(8,128)S(1)} custom-call(f32[48,384]{1,0:T(8,128)S(1)} %pad_maximum_fusion.block_ref, f32[256]{0:T(256)S(1)} %copy-done), custom_call_target="tpu_custom_call" | custom-call | tf_op jit(solution)/shard_map/pallas_call | solution.py:219
  20.6 0.6 %copy.6 = f32[48,256]{1,0:T(8,128)} copy(f32[48,256]{1,0:T(8,128)S(1)} %shard_map.46) | data formatting | bytes 98304
Async XLA Ops:
  0.0 0.9 %copy-start = (f32[256]{0:T(256)S(1)}, f32[256]{0:T(256)}, u32[]{:S(2)}) copy-start(f32[256]{0:T(256)} %scale_ref.1) | copy-start | bytes 3076

commit v4 on v3

v4 whole, which is shorter than its diff:
```python
import functools
import math

import jax
import jax.numpy as jnp
from jax import lax
from jax.experimental import pallas as pl
from jax.experimental.pallas import tpu as pltpu
from jax.sharding import PartitionSpec as P

MESH = pl.DeviceIdType.MESH
LAST = (((1,), (1,)), ((), ()))
FIRST = (((1,), (0,)), ((), ()))


def split(count):
    return max(part for part in range(1, math.isqrt(count) + 1) if count % part == 0)


def dot(left, right, dims):
    return lax.dot_general(left, right, dims, preferred_element_type=jnp.float32)


def halves(value):
    hi = value.astype(jnp.bfloat16)
    return hi, (value - hi.astype(jnp.float32)).astype(jnp.bfloat16)


def ends(square, side):
    lane = lax.broadcasted_iota(jnp.int32, (square.shape[0], 128), 1)
    rest, lanes = -0.5 * square, jnp.where(lane < 6, 1.0, 0.0)
    for index in range(3):
        piece = rest.astype(jnp.bfloat16).astype(jnp.float32)
        lanes = jnp.where(lane == 3 * side + index, piece, lanes)
        rest = rest - piece
    return lanes.astype(jnp.bfloat16)


def kernel(
    sizes,
    block_ref,
    scale_ref,
    out_ref,
    row_buf,
    col_buf,
    part,
    landed,
    row_send,
    row_recv,
    col_send,
    col_recv,
    twin_send,
    twin_recv,
    red_send,
    red_recv,
):
    n_core, n_a, n_b, n_c, n_d = sizes
    points, width = out_ref.shape
    rank = (block_ref.shape[1] - width) // 2
    row, col = lax.axis_index("row"), lax.axis_index("col")
    core, chip = lax.rem(row, n_core), lax.div(row, n_core)
    a, c = lax.rem(chip, n_a), lax.div(chip, n_a)
    b, d = lax.rem(col, n_b), lax.div(col, n_b)

    def device(da=0, db=0, dc=0, dd=0, dcore=0):
        to_chip = lax.rem(c + dc, n_c) * n_a + lax.rem(a + da, n_a)
        to_row = to_chip * n_core + lax.rem(core + dcore, n_core)
        return (to_row, lax.rem(d + dd, n_d) * n_b + lax.rem(b + db, n_b))

    order = [(0, 0)] + [(0, j) for j in range(1, n_b)] + [(i, 0) for i in range(1, n_a)]
    early = len(order)
    order += [(i, j) for i in range(1, n_a) for j in range(1, n_b)]

    def row_slot(da, db):
        return order.index((da, db))

    def col_slot(dc, dd):
        return dc * n_d + dd

    n_row, n_col = n_a * n_b, n_c * n_d
    peers = [device(da=i, db=j) for i in range(n_a) for j in range(n_b) if i + j > 0]
    peers += [device(dc=i) for i in range(1, n_c)]
    peers += [device(dd=i) for i in range(1, n_d)]
    peers += [device(dcore=i) for i in range(1, n_core)]
    barrier = pltpu.get_barrier_semaphore()
    for peer in peers:
        pl.semaphore_signal(barrier, inc=1, device_id=peer, device_id_type=MESH)

    pl.semaphore_wait(barrier, len(peers))

    def remote(src, dst, send, recv, to):
        return pltpu.make_async_remote_copy(
            src_ref=src, dst_ref=dst, send_sem=send, recv_sem=recv, device_id=to, device_id_type=MESH
        )

    pieces = row_send.shape[1]
    piece = points // pieces

    def in_pieces(src, dst, send, recv, to):
        cuts = [pl.ds(index * piece, piece) for index in range(pieces)]
        return [
            remote(src.at[cut], dst.at[cut], send.at[index], recv.at[index], to)
            for index, cut in enumerate(cuts)
        ]

    def row_copy(i, j, by):
        src = block_ref if (i, j) in ((by, 0), (0, by)) else row_buf.at[row_slot(0, j)]
        to = device(da=n_a - by) if i else device(db=n_b - by)
        dst = row_slot(i, j)
        return in_pieces(src, row_buf.at[dst], row_send.at[dst], row_recv.at[dst], to)

    def col_copy(i, j, by):
        src = block_ref if (i, j) in ((by, 0), (0, by)) else col_buf.at[col_slot(0, j)]
        to = device(dc=n_c - by) if i else device(dd=n_d - by)
        dst = col_slot(i, j)
        return in_pieces(src, col_buf.at[dst], col_send.at[dst], col_recv.at[dst], to)

    def twin_copy(slot):
        src = col_buf.at[slot] if slot else block_ref
        dst = col_buf.at[n_col + slot]
        return in_pieces(src, dst, twin_send.at[slot], twin_recv.at[slot], device(dcore=1))

    near = [row_copy(0, j, j) for j in range(1, n_b)]
    far = [col_copy(0, j, j) for j in range(1, n_d)]
    side = [[row_copy(i, j, i) for i in range(1, n_a)] for j in range(n_b)]
    over = [[col_copy(i, j, i) for i in range(1, n_c)] for j in range(n_d)]
    twin = [twin_copy(slot) for slot in range(n_col)] if n_core > 1 else []

    def start(copies, index):
        for copy in copies:
            copy[index].start()

    steps = range(pieces)
    for copies in (far, over[0], side[0], twin[:1], near):
        for index in steps:
            start(copies, index)
    row_buf[0] = block_ref[...]
    col_buf[0] = block_ref[...]

    def pass_far(index):
        for j, copy in enumerate(far, 1):
            copy[index].wait_recv()
            start(over[j], index)
            start(twin[j : j + 1], index)

    def pass_over(j, index):
        for i, copy in enumerate(over[j], 1):
            copy[index].wait_recv()
            start(twin[col_slot(i, j) : col_slot(i, j) + 1], index)

    for index in steps:
        pass_far(index)
        pass_over(0, index)
    for index in steps:
        for j, copy in enumerate(near, 1):
            copy[index].wait_recv()
            start(side[j], index)
        for j in range(1, n_d):
            pass_over(j, index)
    for copy in side[0]:
        for index in steps:
            copy[index].wait_recv()

    scale = scale_ref[...].reshape(1, width)

    def row_side(first, last):
        rows = row_buf[first:last].reshape((last - first) * points, width + 2 * rank)
        row_x, row_uv = rows[:, :width], rows[:, width:]
        row_sq = jnp.sum(row_x * scale * row_x, axis=1, keepdims=True)
        hi, lo = halves(row_x)
        left = jnp.concatenate([hi, lo, hi, ends(row_sq, 1)], axis=1)
        vu_hi, vu_lo = halves(jnp.concatenate([row_uv[:, rank:], row_uv[:, :rank]], axis=1))
        return row_x, left, jnp.concatenate([vu_hi, vu_lo, vu_hi], axis=1)

    def col_side(core_slot):
        cols = col_buf[core_slot * n_col : (core_slot + 1) * n_col]
        cols = cols.reshape(n_col * points, width + 2 * rank)
        col_x = cols[:, :width]
        col_scaled = col_x * scale
        col_sq = jnp.sum(col_scaled * col_x, axis=1, keepdims=True)
        hi, lo = halves(col_scaled)
        right = jnp.concatenate([hi, hi, lo, ends(col_sq, 0)], axis=1)
        uv_hi, uv_lo = halves(cols[:, width:])
        return halves(col_x), right, jnp.concatenate([uv_hi, uv_hi, uv_lo], axis=1)

    def tile(row_terms, col_terms):
        (_, left, vu_left), ((x_hi, x_lo), right, uv_right) = row_terms, col_terms
        coupling = dot(vu_left, uv_right, LAST) * jnp.exp(dot(left, right, LAST))
        hi, lo = halves(coupling)
        both = dot(jnp.concatenate([hi, lo], axis=0), x_hi, FIRST)
        count = left.shape[0]
        pulled = both[:count] + both[count:] + dot(hi, x_lo, FIRST)
        return coupling, pulled, jnp.sum(coupling, axis=1, keepdims=True)

    def finish(first, last, row_x, pulled, sums):
        part[first:last] = (pulled - sums * row_x).reshape(last - first, points, width)
        for slot in range(max(first, 1), last):
            i, j = order[slot]
            to = device(da=i, db=j)
            copy = remote(
                part.at[slot], landed.at[slot], red_send.at[slot], red_recv.at[slot], to
            )
            copy.start()
            reduces.append(copy)

    reduces = []
    row_terms = row_side(0, early)
    row_x = row_terms[0]
    col_terms = [col_side(0)]
    coupling, pulled, sums = tile(row_terms, col_terms[0])
    place = [lax.broadcasted_iota(jnp.int32, (points, n_col * points), axis) for axis in (0, 1)]
    diagonal = jnp.where(place[0] == place[1], coupling[:points], 0.0)
    diagonal = jnp.sum(diagonal, axis=1, keepdims=True)
    diag_hi, diag_lo = (half.astype(jnp.float32) for half in halves(diagonal))
    own = row_x[:points]
    own_hi, own_lo = (half.astype(jnp.float32) for half in halves(own))
    rest = diagonal * own - diag_hi * own_hi - diag_hi * own_lo - diag_lo * own_hi

    for copy in twin:
        for index in steps:
            copy[index].wait_recv()
    for core_slot in range(1, n_core):
        col_terms.append(col_side(core_slot))
        _, more_pulled, more_sums = tile(row_terms, col_terms[core_slot])
        pulled, sums = pulled + more_pulled, sums + more_sums
    finish(0, early, row_x, pulled, sums)

    if early < n_row:
        for copies in side[1:]:
            for copy in copies:
                for index in steps:
                    copy[index].wait_recv()
        row_terms = row_side(early, n_row)
        results = [tile(row_terms, terms) for terms in col_terms]
        finish(
            early,
            n_row,
            row_terms[0],
            sum(result[1] for result in results),
            sum(result[2] for result in results),
        )
    total = part[0] + rest
    for slot, copy in enumerate(reduces, 1):
        copy.wait_recv()
        total = total + landed[slot]
    out_ref[...] = total * scale

    for copies in (near, far, *side, *over, twin):
        for copy in copies:
            for index in steps:
                copy[index].wait_send()
    for copy in reduces:
        copy.wait_send()


def on_device(sizes, features, inv_scale, probe_u, solve_v):
    n_core, n_a, n_b, n_c, n_d = sizes
    points, width = features.shape
    rank = probe_u.shape[1]
    n_row, n_col = n_a * n_b, n_c * n_d
    pieces = 2 if points % 16 == 0 else 1
    f32, dma = jnp.float32, pltpu.SemaphoreType.DMA
    return pl.pallas_call(
        functools.partial(kernel, sizes),
        out_shape=jax.ShapeDtypeStruct((points, width), f32),
        in_specs=[pl.BlockSpec(memory_space=pltpu.VMEM)] * 2,
        out_specs=pl.BlockSpec(memory_space=pltpu.VMEM),
        scratch_shapes=[
            pltpu.VMEM((n_row, points, width + 2 * rank), f32),
            pltpu.VMEM((n_core * n_col, points, width + 2 * rank), f32),
            pltpu.VMEM((n_row, points, width), f32),
            pltpu.VMEM((n_row, points, width), f32),
            dma((n_row, pieces)),
            dma((n_row, pieces)),
            dma((n_col, pieces)),
            dma((n_col, pieces)),
            dma((n_col, pieces)),
            dma((n_col, pieces)),
            dma((n_row,)),
            dma((n_row,)),
        ],
        compiler_params=pltpu.CompilerParams(
            collective_id=0, has_side_effects=True, vmem_limit_bytes=48 * 2**20
        ),
    )(jnp.concatenate([features, probe_u, solve_v], axis=1), inv_scale)


def solution(mesh):
    rows, cols = mesh.shape["row"], mesh.shape["col"]
    n_core = 2 if rows % 2 == 0 else 1
    chips = rows // n_core
    n_a, n_b = split(chips), split(cols)
    sizes = (n_core, n_a, n_b, chips // n_a, cols // n_b)
    return jax.shard_map(
        functools.partial(on_device, sizes),
        mesh=mesh,
        in_specs=(P(("row", "col"), None), P(), P(("row", "col"), None), P(("row", "col"), None)),
        out_specs=P(("row", "col"), None),
        check_vma=False,
    )
```

time: 21.4 us -> 21.5 us (level)
  no operation moved by 1% of the time
where the time goes in v4:
time: 21.5 us; the launch traced here: 21.3 us
  Pallas kernels  19.8 us (92%)
  other arithmetic  0.92 us (4%)
  local copies, waits for them, and re-layouts  0.63 us (3%)
    pallas_call x1, Pallas kernels, on_device(): pl.pallas_call(functools.partial(kernel, sizes), out_shape=jax.ShapeDtype...  19.8 us
    concatenate x1, other arithmetic, on_device(): jnp.concatenate([features, probe_u, solve_v], axis=1)  0.92 us
    unnamed x3, local copies, waits for them, and re-layouts  0.63 us

profile of v4, /device:TPU:0, one launch (start us, length us, event | category | flops | bytes accessed | tf_op | source)
XLA Modules:
  0.0 21.3 jit_solution(5121014221892671128)
XLA Ops:
  0.0 0.0 copy-start
  0.0 0.9 %pad_maximum_fusion.block_ref = f32[48,384]{1,0:T(8,128)S(1)} fusion(f32[48,64]{1,0:T(8,128)} %param.7, f32[48,64]{1,0:T(8,128)} %param.6, f32[48,256]{1,0:T(8,128)} %param.4), kind=kLoop, calls=%fused_computation | loop fusion | flops 36864 | bytes 147456 | tf_op jit(solution)/shard_map/concatenate | solution.py:285
  0.9 0.0 copy-done
  0.9 19.8 %shard_map.46 = f32[48,256]{1,0:T(8,128)S(1)} custom-call(f32[48,384]{1,0:T(8,128)S(1)} %pad_maximum_fusion.block_ref, f32[256]{0:T(256)S(1)} %copy-done), custom_call_target="tpu_custom_call" | custom-call | tf_op jit(solution)/shard_map/pallas_call | solution.py:263
  20.7 0.6 %copy.6 = f32[48,256]{1,0:T(8,128)} copy(f32[48,256]{1,0:T(8,128)S(1)} %shard_map.46) | data formatting | bytes 98304
Async XLA Ops:
  0.0 0.9 %copy-start = (f32[256]{0:T(256)S(1)}, f32[256]{0:T(256)}, u32[]{:S(2)}) copy-start(f32[256]{0:T(256)} %scale_ref.1) | copy-start | bytes 3076

commit v5 on v4

--- a/solution.py
+++ b/solution.py
@@ -62,10 +62,15 @@
     a, c = lax.rem(chip, n_a), lax.div(chip, n_a)
     b, d = lax.rem(col, n_b), lax.div(col, n_b)
 
+    def around(own, count):
+        return [own] + [lax.rem(own + step, count) for step in range(1, count)]
+
+    cores, cs = around(core, n_core), [n_a * n_core * at for at in around(c, n_c)]
+    rows_at = [n_core * at for at in around(a, n_a)]
+    bs, ds = around(b, n_b), [n_b * at for at in around(d, n_d)]
+
     def device(da=0, db=0, dc=0, dd=0, dcore=0):
-        to_chip = lax.rem(c + dc, n_c) * n_a + lax.rem(a + da, n_a)
-        to_row = to_chip * n_core + lax.rem(core + dcore, n_core)
-        return (to_row, lax.rem(d + dd, n_d) * n_b + lax.rem(b + db, n_b))
+        return (cs[dc] + rows_at[da] + cores[dcore], ds[dd] + bs[db])
 
     order = [(0, 0)] + [(0, j) for j in range(1, n_b)] + [(i, 0) for i in range(1, n_a)]
     early = len(order)
@@ -94,31 +99,33 @@
         )
 
     pieces = row_send.shape[1]
-    piece = points // pieces
-
-    def in_pieces(src, dst, send, recv, to):
-        cuts = [pl.ds(index * piece, piece) for index in range(pieces)]
+
+    def in_pieces(count, src, dst, send, recv, to):
+        size = points // count
+        cuts = [pl.ds(index * size, size) for index in range(count)]
         return [
             remote(src.at[cut], dst.at[cut], send.at[index], recv.at[index], to)
             for index, cut in enumerate(cuts)
         ]
 
     def row_copy(i, j, by):
-        src = block_ref if (i, j) in ((by, 0), (0, by)) else row_buf.at[row_slot(0, j)]
+        direct = j == 0
+        src = block_ref if direct or i == 0 else row_buf.at[row_slot(0, j)]
         to = device(da=n_a - by) if i else device(db=n_b - by)
-        dst = row_slot(i, j)
-        return in_pieces(src, row_buf.at[dst], row_send.at[dst], row_recv.at[dst], to)
+        dst, count = row_slot(i, j), 1 if direct else pieces
+        return in_pieces(count, src, row_buf.at[dst], row_send.at[dst], row_recv.at[dst], to)
 
     def col_copy(i, j, by):
-        src = block_ref if (i, j) in ((by, 0), (0, by)) else col_buf.at[col_slot(0, j)]
+        direct = j == 0
+        src = block_ref if direct or i == 0 else col_buf.at[col_slot(0, j)]
         to = device(dc=n_c - by) if i else device(dd=n_d - by)
-        dst = col_slot(i, j)
-        return in_pieces(src, col_buf.at[dst], col_send.at[dst], col_recv.at[dst], to)
+        dst, count = col_slot(i, j), 1 if direct else pieces
+        return in_pieces(count, src, col_buf.at[dst], col_send.at[dst], col_recv.at[dst], to)
 
     def twin_copy(slot):
         src = col_buf.at[slot] if slot else block_ref
         dst = col_buf.at[n_col + slot]
-        return in_pieces(src, dst, twin_send.at[slot], twin_recv.at[slot], device(dcore=1))
+        return in_pieces(1, src, dst, twin_send.at[slot], twin_recv.at[slot], device(dcore=1))
 
     near = [row_copy(0, j, j) for j in range(1, n_b)]
     far = [col_copy(0, j, j) for j in range(1, n_d)]
@@ -126,40 +133,40 @@
     over = [[col_copy(i, j, i) for i in range(1, n_c)] for j in range(n_d)]
     twin = [twin_copy(slot) for slot in range(n_col)] if n_core > 1 else []
 
-    def start(copies, index):
+    def start(copies):
         for copy in copies:
-            copy[index].start()
-
-    steps = range(pieces)
-    for copies in (far, over[0], side[0], twin[:1], near):
-        for index in steps:
-            start(copies, index)
+            copy.start()
+
+    def arrive(copies):
+        for copy in copies:
+            copy.wait_recv()
+
+    def start_twin(i, j):
+        if n_core > 1:
+            start(twin[col_slot(i, j)])
+
+    for index in range(pieces):
+        start([copy[index] for copy in far + near])
+    for copy in over[0] + side[0] + twin[:1]:
+        start(copy)
     row_buf[0] = block_ref[...]
     col_buf[0] = block_ref[...]
 
-    def pass_far(index):
+    for index in range(pieces):
         for j, copy in enumerate(far, 1):
             copy[index].wait_recv()
-            start(over[j], index)
-            start(twin[j : j + 1], index)
-
-    def pass_over(j, index):
-        for i, copy in enumerate(over[j], 1):
-            copy[index].wait_recv()
-            start(twin[col_slot(i, j) : col_slot(i, j) + 1], index)
-
-    for index in steps:
-        pass_far(index)
-        pass_over(0, index)
-    for index in steps:
+            start([relay[index] for relay in over[j]])
         for j, copy in enumerate(near, 1):
             copy[index].wait_recv()
-            start(side[j], index)
-        for j in range(1, n_d):
-            pass_over(j, index)
+            start([relay[index] for relay in side[j]])
+    for j in range(1, n_d):
+        start_twin(0, j)
+    for j in range(n_d):
+        for i, copy in enumerate(over[j], 1):
+            arrive(copy)
+            start_twin(i, j)
     for copy in side[0]:
-        for index in steps:
-            copy[index].wait_recv()
+        arrive(copy)
 
     scale = scale_ref[...].reshape(1, width)
 
@@ -217,8 +224,7 @@
     rest = diagonal * own - diag_hi * own_hi - diag_hi * own_lo - diag_lo * own_hi
 
     for copy in twin:
-        for index in steps:
-            copy[index].wait_recv()
+        arrive(copy)
     for core_slot in range(1, n_core):
         col_terms.append(col_side(core_slot))
         _, more_pulled, more_sums = tile(row_terms, col_terms[core_slot])
@@ -228,8 +234,7 @@
     if early < n_row:
         for copies in side[1:]:
             for copy in copies:
-                for index in steps:
-                    copy[index].wait_recv()
+                arrive(copy)
         row_terms = row_side(early, n_row)
         results = [tile(row_terms, terms) for terms in col_terms]
         finish(
@@ -247,8 +252,8 @@
 
     for copies in (near, far, *side, *over, twin):
         for copy in copies:
-            for index in steps:
-                copy[index].wait_send()
+            for part_copy in copy:
+                part_copy.wait_send()
     for copy in reduces:
         copy.wait_send()
 
@@ -274,8 +279,8 @@
             dma((n_row, pieces)),
             dma((n_col, pieces)),
             dma((n_col, pieces)),
-            dma((n_col, pieces)),
-            dma((n_col, pieces)),
+            dma((n_col, 1)),
+            dma((n_col, 1)),
             dma((n_row,)),
             dma((n_row,)),
         ],

time: 21.5 us -> 21.2 us (0.986)
  Pallas kernels: 19.8 us -> 19.4 us
    pallas_call x1, Pallas kernels: 19.8 us -> 19.4 us  [on_device(): pl.pallas_call(functools.partial(kernel, sizes), out_shape=jax.ShapeDtype...]
where the time goes in v5:
time: 21.2 us; the launch traced here: 21 us
  Pallas kernels  19.4 us (92%)
  other arithmetic  0.92 us (4%)
  local copies, waits for them, and re-layouts  0.63 us (3%)
    pallas_call x1, Pallas kernels, on_device(): pl.pallas_call(functools.partial(kernel, sizes), out_shape=jax.ShapeDtype...  19.4 us
    concatenate x1, other arithmetic, on_device(): jnp.concatenate([features, probe_u, solve_v], axis=1)  0.92 us
    unnamed x3, local copies, waits for them, and re-layouts  0.63 us

profile of v5, /device:TPU:0, one launch (start us, length us, event | category | flops | bytes accessed | tf_op | source)
XLA Modules:
  0.0 21.0 jit_solution(16407242995649383293)
XLA Ops:
  0.0 0.0 copy-start
  0.0 0.9 %pad_maximum_fusion.block_ref = f32[48,384]{1,0:T(8,128)S(1)} fusion(f32[48,64]{1,0:T(8,128)} %param.7, f32[48,64]{1,0:T(8,128)} %param.6, f32[48,256]{1,0:T(8,128)} %param.4), kind=kLoop, calls=%fused_computation | loop fusion | flops 36864 | bytes 147456 | tf_op jit(solution)/shard_map/concatenate | solution.py:290
  0.9 0.0 copy-done
  0.9 19.4 %shard_map.46 = f32[48,256]{1,0:T(8,128)S(1)} custom-call(f32[48,384]{1,0:T(8,128)S(1)} %pad_maximum_fusion.block_ref, f32[256]{0:T(256)S(1)} %copy-done), custom_call_target="tpu_custom_call" | custom-call | tf_op jit(solution)/shard_map/pallas_call | solution.py:268
  20.4 0.6 %copy.6 = f32[48,256]{1,0:T(8,128)} copy(f32[48,256]{1,0:T(8,128)S(1)} %shard_map.46) | data formatting | bytes 98304
Async XLA Ops:
  0.0 0.9 %copy-start = (f32[256]{0:T(256)S(1)}, f32[256]{0:T(256)}, u32[]{:S(2)}) copy-start(f32[256]{0:T(256)} %scale_ref.1) | copy-start | bytes 3076

commit v6 on v5

--- a/solution.py
+++ b/solution.py
@@ -38,9 +38,16 @@
 
 def kernel(
     sizes,
+    x_ref,
+    scale_ref,
+    u_ref,
+    v_ref,
+    out_ref,
     block_ref,
-    scale_ref,
-    out_ref,
+    scale_buf,
+    u_buf,
+    v_buf,
+    local_sem,
     row_buf,
     col_buf,
     part,
@@ -91,6 +98,17 @@
     for peer in peers:
         pl.semaphore_signal(barrier, inc=1, device_id=peer, device_id_type=MESH)
 
+    loads = [
+        pltpu.make_async_copy(x_ref, block_ref.at[:, pl.ds(0, width)], local_sem.at[0]),
+        pltpu.make_async_copy(u_ref, u_buf, local_sem.at[1]),
+        pltpu.make_async_copy(v_ref, v_buf, local_sem.at[2]),
+        pltpu.make_async_copy(scale_ref, scale_buf, local_sem.at[3]),
+    ]
+    for load in loads:
+        load.start()
+    for load in loads[:3]:
+        load.wait()
+    block_ref[:, width:] = jnp.concatenate([u_buf[...], v_buf[...]], axis=1)
     pl.semaphore_wait(barrier, len(peers))
 
     def remote(src, dst, send, recv, to):
@@ -168,7 +186,8 @@
     for copy in side[0]:
         arrive(copy)
 
-    scale = scale_ref[...].reshape(1, width)
+    loads[3].wait()
+    scale = scale_buf[...].reshape(1, width)
 
     def row_side(first, last):
         rows = row_buf[first:last].reshape((last - first) * points, width + 2 * rank)
@@ -268,9 +287,14 @@
     return pl.pallas_call(
         functools.partial(kernel, sizes),
         out_shape=jax.ShapeDtypeStruct((points, width), f32),
-        in_specs=[pl.BlockSpec(memory_space=pltpu.VMEM)] * 2,
+        in_specs=[pl.BlockSpec(memory_space=pltpu.HBM)] * 4,
         out_specs=pl.BlockSpec(memory_space=pltpu.VMEM),
         scratch_shapes=[
+            pltpu.VMEM((points, width + 2 * rank), f32),
+            pltpu.VMEM((width,), f32),
+            pltpu.VMEM((points, rank), f32),
+            pltpu.VMEM((points, rank), f32),
+            dma((4,)),
             pltpu.VMEM((n_row, points, width + 2 * rank), f32),
             pltpu.VMEM((n_core * n_col, points, width + 2 * rank), f32),
             pltpu.VMEM((n_row, points, width), f32),
@@ -287,7 +311,7 @@
         compiler_params=pltpu.CompilerParams(
             collective_id=0, has_side_effects=True, vmem_limit_bytes=48 * 2**20
         ),
-    )(jnp.concatenate([features, probe_u, solve_v], axis=1), inv_scale)
+    )(*(pltpu.with_memory_space_constraint(x, pltpu.HBM) for x in (features, inv_scale, probe_u, solve_v)))
 
 
 def solution(mesh):

time: 21.2 us -> 20.4 us (0.962)
  other arithmetic: 0.92 us -> 0 us
    concatenate x1 -> x0, other arithmetic: 0.92 us -> none  [on_device(): jnp.concatenate([features, probe_u, solve_v], axis=1)]
    unnamed x3 -> x1, local copies, waits for them, and re-layouts: 0.63 us -> 0.62 us
where the time goes in v6:
time: 20.4 us; the launch traced here: 20.3 us
  Pallas kernels  19.6 us (96%)
  local copies, waits for them, and re-layouts  0.62 us (3%)
    pallas_call x1, Pallas kernels, on_device(): pl.pallas_call(functools.partial(kernel, sizes), out_shape=jax.ShapeDtype...  19.6 us
    unnamed x1, local copies, waits for them, and re-layouts  0.62 us

profile of v6, /device:TPU:0, one launch (start us, length us, event | category | flops | bytes accessed | tf_op | source)
XLA Modules:
  0.0 20.3 jit_solution(16088905755369661185)
XLA Ops:
  0.0 19.6 %shard_map.46 = f32[48,256]{1,0:T(8,128)S(1)} custom-call(f32[48,256]{1,0:T(8,128)} %x_ref.1, f32[256]{0:T(256)} %scale_ref.1, f32[48,64]{1,0:T(8,128)} %u_ref.1, f32[48,64]{1,0:T(8,128)} %v_ref.1), custom_call_target="tpu_custom_call" | custom-call | tf_op jit(solution)/shard_map/pallas_call | solution.py:287
  19.6 0.6 %copy.6 = f32[48,256]{1,0:T(8,128)} copy(f32[48,256]{1,0:T(8,128)S(1)} %shard_map.46) | data formatting | bytes 98304

commit v7 on v6

--- a/solution.py
+++ b/solution.py
@@ -91,8 +91,7 @@
 
     n_row, n_col = n_a * n_b, n_c * n_d
     peers = [device(da=i, db=j) for i in range(n_a) for j in range(n_b) if i + j > 0]
-    peers += [device(dc=i) for i in range(1, n_c)]
-    peers += [device(dd=i) for i in range(1, n_d)]
+    peers += [device(dc=i, dd=j) for i in range(n_c) for j in range(n_d) if i + j > 0]
     peers += [device(dcore=i) for i in range(1, n_core)]
     barrier = pltpu.get_barrier_semaphore()
     for peer in peers:
@@ -133,12 +132,9 @@
         dst, count = row_slot(i, j), 1 if direct else pieces
         return in_pieces(count, src, row_buf.at[dst], row_send.at[dst], row_recv.at[dst], to)
 
-    def col_copy(i, j, by):
-        direct = j == 0
-        src = block_ref if direct or i == 0 else col_buf.at[col_slot(0, j)]
-        to = device(dc=n_c - by) if i else device(dd=n_d - by)
-        dst, count = col_slot(i, j), 1 if direct else pieces
-        return in_pieces(count, src, col_buf.at[dst], col_send.at[dst], col_recv.at[dst], to)
+    def col_copy(i, j):
+        dst, to = col_slot(i, j), device(dc=(n_c - i) % n_c, dd=(n_d - j) % n_d)
+        return remote(block_ref, col_buf.at[dst], col_send.at[dst], col_recv.at[dst], to)
 
     def twin_copy(slot):
         src = col_buf.at[slot] if slot else block_ref
@@ -146,9 +142,9 @@
         return in_pieces(1, src, dst, twin_send.at[slot], twin_recv.at[slot], device(dcore=1))
 
     near = [row_copy(0, j, j) for j in range(1, n_b)]
-    far = [col_copy(0, j, j) for j in range(1, n_d)]
     side = [[row_copy(i, j, i) for i in range(1, n_a)] for j in range(n_b)]
-    over = [[col_copy(i, j, i) for i in range(1, n_c)] for j in range(n_d)]
+    cols = [(i, j) for i in range(n_c) for j in range(n_d) if i + j > 0]
+    over = {(i, j): col_copy(i, j) for i, j in cols}
     twin = [twin_copy(slot) for slot in range(n_col)] if n_core > 1 else []
 
     def start(copies):
@@ -163,26 +159,24 @@
         if n_core > 1:
             start(twin[col_slot(i, j)])
 
+    apart = [at for at in cols if 0 not in at]
+    direct = [at for at in cols if 0 in at]
+    start([over[at] for at in apart])
     for index in range(pieces):
-        start([copy[index] for copy in far + near])
-    for copy in over[0] + side[0] + twin[:1]:
+        start([copy[index] for copy in near])
+    start([over[at] for at in direct])
+    for copy in side[0] + twin[:1]:
         start(copy)
     row_buf[0] = block_ref[...]
     col_buf[0] = block_ref[...]
 
     for index in range(pieces):
-        for j, copy in enumerate(far, 1):
-            copy[index].wait_recv()
-            start([relay[index] for relay in over[j]])
         for j, copy in enumerate(near, 1):
             copy[index].wait_recv()
             start([relay[index] for relay in side[j]])
-    for j in range(1, n_d):
-        start_twin(0, j)
-    for j in range(n_d):
-        for i, copy in enumerate(over[j], 1):
-            arrive(copy)
-            start_twin(i, j)
+    for at in direct + apart:
+        over[at].wait_recv()
+        start_twin(*at)
     for copy in side[0]:
         arrive(copy)
 
@@ -269,10 +263,12 @@
         total = total + landed[slot]
     out_ref[...] = total * scale
 
-    for copies in (near, far, *side, *over, twin):
+    for copies in (near, *side, twin):
         for copy in copies:
             for part_copy in copy:
                 part_copy.wait_send()
+    for copy in over.values():
+        copy.wait_send()
     for copy in reduces:
         copy.wait_send()
 
@@ -301,8 +297,8 @@
             pltpu.VMEM((n_row, points, width), f32),
             dma((n_row, pieces)),
             dma((n_row, pieces)),
-            dma((n_col, pieces)),
-            dma((n_col, pieces)),
+            dma((n_col,)),
+            dma((n_col,)),
             dma((n_col, 1)),
             dma((n_col, 1)),
             dma((n_row,)),

time: 20.4 us -> 19.9 us (0.975)
  Pallas kernels: 19.6 us -> 19.1 us
    pallas_call x1, Pallas kernels: 19.6 us -> 19.1 us  [on_device(): pl.pallas_call(functools.partial(kernel, sizes), out_shape=jax.ShapeDtype...]
where the time goes in v7:
time: 19.9 us; the launch traced here: 19.7 us
  Pallas kernels  19.1 us (96%)
  local copies, waits for them, and re-layouts  0.62 us (3%)
    pallas_call x1, Pallas kernels, on_device(): pl.pallas_call(functools.partial(kernel, sizes), out_shape=jax.ShapeDtype...  19.1 us
    unnamed x1, local copies, waits for them, and re-layouts  0.62 us

profile of v7, /device:TPU:0, one launch (start us, length us, event | category | flops | bytes accessed | tf_op | source)
XLA Modules:
  0.0 19.7 jit_solution(8433717395395417756)
XLA Ops:
  0.0 19.1 %shard_map.46 = f32[48,256]{1,0:T(8,128)S(1)} custom-call(f32[48,256]{1,0:T(8,128)} %x_ref.1, f32[256]{0:T(256)} %scale_ref.1, f32[48,64]{1,0:T(8,128)} %u_ref.1, f32[48,64]{1,0:T(8,128)} %v_ref.1), custom_call_target="tpu_custom_call" | custom-call | tf_op jit(solution)/shard_map/pallas_call | solution.py:283
  19.1 0.6 %copy.6 = f32[48,256]{1,0:T(8,128)} copy(f32[48,256]{1,0:T(8,128)S(1)} %shard_map.46) | data formatting | bytes 98304
